TPU v7x, 32 devices: a whole 2x2x4 slice. The times are simulated.
32 devices in a mesh: grp: 4 (over y, x), line: 8 (over z, core).
Axes of the slice: x: 2, y: 2, z: 4, core: 2. Of those that a mesh axis runs over, the one named last changes fastest.
Arguments:
- adjoint: float32 [5, 16, 1024, 1024], P(None, 'grp', 'line'), may hold values from -6 to 6
- source: float32 [5, 16, 1024, 1024], P(None, 'grp', 'line'), may hold values from -6 to 6
- jacobian: float32 [3, 5, 5], replicated, may hold values from -2.5 to 2.5
- inverse_x: float32 [1024, 1024], replicated, may hold values from 0 to 3
- inverse_y: float32 [1024, 1024], replicated, may hold values from 0 to 3
- inverse_z: float32 [16, 16], replicated, may hold values from 0 to 3
Outputs:
- update: float32 [5, 16, 1024, 1024], P(None, 'grp', 'line')
All inputs are finite; a program needn't handle non-finite values.
Results may differ from a plain program's by a relative error of at most 0.00011.
Values sent between devices are 32-bit elements; how exact they have to be, the bound alone decides.
A program may use at most 256 MiB of HBM per device.

v0:
```python
import functools

import jax
import jax.numpy as jnp
from jax import lax
from jax.experimental import pallas as pl
from jax.experimental.pallas import tpu as pltpu
from jax.sharding import PartitionSpec as P

dissipation = 0.05
highest = lax.Precision.HIGHEST


def padded_2(cells, sides, width):
    for axis, dim in sides:
        count = lax.axis_size(axis)
        ends = count - 1
        head = lax.slice_in_dim(cells, 0, width, axis=dim)
        tail = lax.slice_in_dim(cells, cells.shape[dim] - width, cells.shape[dim], axis=dim)
        cells = jnp.concatenate(
            [
                lax.ppermute(tail, axis, [(i, (i + 1) % count) for i in range(ends)]),
                cells,
                lax.ppermute(head, axis, [((i + 1) % count, i) for i in range(ends)]),
            ],
            axis=dim,
        )
    return cells


def shift_last(field, offset):
    if offset == 0:
        return field
    zeros = jnp.zeros(field.shape[:-1] + (abs(offset),), field.dtype)
    if offset > 0:
        return jnp.concatenate([field[..., offset:], zeros], axis=-1)
    return jnp.concatenate([zeros, field[..., :offset]], axis=-1)


def stencil_sum(padded, source, jacobian):
    components = source.shape[0]
    depth = source.shape[1]
    rows_local = source.shape[2]

    def window(step_z, step_y, step_x):
        inner = padded[:, 2 + step_z : 2 + step_z + depth, 2 + step_y : 2 + step_y + rows_local, :]
        return shift_last(inner, step_x)

    centre = window(0, 0, 0)
    units = ((1, 0, 0), (0, 1, 0), (0, 0, 1))
    damping = jnp.zeros_like(source)
    centrals = []
    for direction in range(3):
        step_z, step_y, step_x = units[direction]
        forward = window(step_z, step_y, step_x)
        backward = window(-step_z, -step_y, -step_x)
        far_forward = window(2 * step_z, 2 * step_y, 2 * step_x)
        far_backward = window(-2 * step_z, -2 * step_y, -2 * step_x)
        centrals.append(0.5 * (forward - backward))
        damping = damping + (
            far_forward - 4.0 * forward + 6.0 * centre - 4.0 * backward + far_backward
        )
    outputs = []
    for target in range(components):
        total = source[target]
        for direction in range(3):
            for anchor in range(components):
                total = total + jacobian[direction, anchor, target] * centrals[direction][anchor]
        outputs.append(total)
    return jnp.stack(outputs, axis=0) - dissipation * damping


def shards_plain(adjoint, source, jacobian, inverse_x, inverse_y, inverse_z):
    components = adjoint.shape[0]
    depth = adjoint.shape[1]
    rows_local = adjoint.shape[2]
    width = adjoint.shape[3]
    line_count = lax.axis_size("line")
    group_count = lax.axis_size("grp")
    total_y = inverse_y.shape[0]
    total_z = inverse_z.shape[0]
    padded = padded_2(adjoint, (("grp", 1), ("line", 2)), 2)
    residual = stencil_sum(padded, source, jacobian)
    flat = residual.reshape(components * depth * rows_local, width)
    swept = lax.dot_general(inverse_x, flat, (((1,), (1,)), ((), ())), precision=highest)
    block_x = width // line_count
    block_y = total_y // group_count
    sent = swept.reshape(line_count, block_x * components * depth * rows_local)
    lines = lax.all_to_all(sent, "line", split_axis=0, concat_axis=0, tiled=True)
    lines = lines.reshape(line_count, block_x * components * depth, rows_local)
    split_y = inverse_y.reshape(total_y, line_count, rows_local)
    along_y = lax.dot_general(lines, split_y, (((0, 2), (1, 2)), ((), ())), precision=highest)
    along_y = along_y.reshape(block_x * components, depth, group_count, block_y)
    columns = lax.all_to_all(along_y, "grp", split_axis=2, concat_axis=1, tiled=True)
    columns = columns.reshape(block_x * components, total_z, block_y)
    along_z = lax.dot_general(inverse_z, columns, (((1,), (1,)), ((), ())), precision=highest)
    regrouped = lax.all_to_all(along_z, "grp", split_axis=0, concat_axis=2, tiled=True)
    regrouped = regrouped.reshape(depth, block_x, components, line_count, rows_local)
    returned = lax.all_to_all(regrouped, "line", split_axis=3, concat_axis=1, tiled=True)
    returned = returned.reshape(depth, width, components, rows_local)
    return jnp.transpose(returned, (2, 0, 3, 1))


MESH = pl.DeviceIdType.MESH


def halves(values):
    high = values.astype(jnp.bfloat16)
    return high, (values - high.astype(jnp.float32)).astype(jnp.bfloat16)


def split_halves(values):
    high = lax.reduce_precision(values, exponent_bits=8, mantissa_bits=7)
    return high.astype(jnp.bfloat16), (values - high).astype(jnp.bfloat16)


def product(left, right):
    dims = (((1,), (1,)), ((), ()))

    def one(a, b):
        return lax.dot_general(a, b, dims, preferred_element_type=jnp.float32)

    return one(left[0], right[0]) + (one(left[0], right[1]) + one(left[1], right[0]))


def sweep_x_body(high_ref, low_ref, field_ref, out_ref):
    depth, rows, width = field_ref.shape[1:]
    field = halves(field_ref[0].reshape(depth * rows, width))
    swept = product((high_ref[...], low_ref[...]), field)
    for plane in range(depth):
        part = swept[:, plane * rows : (plane + 1) * rows]
        out_ref[0, :, plane] = part.reshape(out_ref.shape[1], out_ref.shape[3], rows)


def sweep_x(high, low, residual, devices):
    components, depth, rows, width = residual.shape
    columns = width // devices
    return pl.pallas_call(
        sweep_x_body,
        grid=(components,),
        in_specs=[
            pl.BlockSpec((width, width), lambda v: (0, 0)),
            pl.BlockSpec((width, width), lambda v: (0, 0)),
            pl.BlockSpec((1, depth, rows, width), lambda v: (v, 0, 0, 0)),
        ],
        out_specs=pl.BlockSpec((1, devices, depth, columns, rows), lambda v: (v, 0, 0, 0, 0)),
        out_shape=jax.ShapeDtypeStruct((components, devices, depth, columns, rows), jnp.float32),
        compiler_params=pltpu.CompilerParams(vmem_limit_bytes=48 * 2**20),
    )(high, low, residual)


def middle_body(
    groups, lines, z_ref, high_ref, low_ref, sent_ref, back_ref,
    got, done, field_high, field_low, lined, send_one, recv_one, send_two, recv_two,
):
    components, devices, depth, columns, rows = sent_ref.shape
    total_z = groups * depth
    own_g = lax.axis_index("grp")
    own_l = lax.axis_index("line")
    own = own_g * lines + own_l

    def partner(step):
        l = lax.rem(own_l + step // groups, lines)
        g = lax.rem(own_g + step % groups, groups)
        return g, l

    barrier = pltpu.get_barrier_semaphore()

    def greet(step, carry):
        g, l = partner(step)
        pl.semaphore_signal(barrier, inc=1, device_id=(g, l), device_id_type=MESH)
        return carry

    lax.fori_loop(1, devices, greet, 0)
    pl.semaphore_wait(barrier, devices - 1)

    def first(v, carry):
        pltpu.make_async_copy(sent_ref.at[v, own], got.at[v, own], recv_one.at[v]).start()

        def one(step, c):
            g, l = partner(step)
            pltpu.make_async_remote_copy(
                src_ref=sent_ref.at[v, g * lines + l],
                dst_ref=got.at[v, own],
                send_sem=send_one.at[v],
                recv_sem=recv_one.at[v],
                device_id=(g, l),
                device_id_type=MESH,
            ).start()
            return c

        lax.fori_loop(1, devices, one, 0)
        return carry

    lax.fori_loop(0, components, first, 0)

    def solve(v, carry):
        pltpu.make_async_copy(got.at[v], got.at[v], recv_one.at[v]).wait()
        for g in range(groups):
            block = jnp.concatenate(
                [got[v, g * lines + l].reshape(depth * columns, rows) for l in range(lines)], axis=-1
            )
            high, low = halves(block)
            field_high[pl.ds(g * depth * columns, depth * columns), :] = high
            field_low[pl.ds(g * depth * columns, depth * columns), :] = low

        def line(i, c):
            l = lax.rem(own_l + i, lines)
            at = pl.ds(pl.multiple_of(l * rows, rows), rows)
            solved = product(
                (field_high[...], field_low[...]), (high_ref[at, :], low_ref[at, :])
            )
            lined[...] = solved.reshape(total_z, columns, rows)
            for q in range(total_z):
                total = z_ref[q, 0] * lined[0]
                for z in range(1, total_z):
                    total = total + z_ref[q, z] * lined[z]
                done[v, (q // depth) * lines + l, q % depth] = total

            def send(j, cc):
                g = lax.rem(own_g + j, groups)
                pltpu.make_async_remote_copy(
                    src_ref=done.at[v, g * lines + l],
                    dst_ref=back_ref.at[v, own],
                    send_sem=send_two.at[v],
                    recv_sem=recv_two.at[v],
                    device_id=(g, l),
                    device_id_type=MESH,
                ).start()
                return cc

            @pl.when(i == 0)
            def _():
                pltpu.make_async_copy(done.at[v, own], back_ref.at[v, own], recv_two.at[v]).start()
                lax.fori_loop(1, groups, send, 0)

            @pl.when(i > 0)
            def _():
                lax.fori_loop(0, groups, send, 0)

            return c

        lax.fori_loop(0, lines, line, 0)
        return carry

    lax.fori_loop(0, components, solve, 0)

    def finish(v, carry):
        others = pl.ds(0, devices - 1)
        pltpu.make_async_copy(sent_ref.at[v, others], sent_ref.at[v, others], send_one.at[v]).wait()
        pltpu.make_async_copy(done.at[v, others], done.at[v, others], send_two.at[v]).wait()
        pltpu.make_async_copy(back_ref.at[v], back_ref.at[v], recv_two.at[v]).wait()
        return carry

    lax.fori_loop(0, components, finish, 0)


def middle(inverse_z, high, low, sent, groups, lines):
    components, devices, depth, columns, rows = sent.shape
    total_y = high.shape[0]
    total_z = groups * depth
    return pl.pallas_call(
        functools.partial(middle_body, groups, lines),
        in_specs=[
            pl.BlockSpec(memory_space=pltpu.SMEM),
            pl.BlockSpec(memory_space=pltpu.VMEM),
            pl.BlockSpec(memory_space=pltpu.VMEM),
            pl.BlockSpec(memory_space=pl.ANY),
        ],
        out_specs=pl.BlockSpec(memory_space=pl.ANY),
        out_shape=jax.ShapeDtypeStruct(sent.shape, jnp.float32),
        scratch_shapes=[
            pltpu.VMEM(sent.shape, jnp.float32),
            pltpu.VMEM(sent.shape, jnp.float32),
            pltpu.VMEM((total_z * columns, total_y), jnp.bfloat16),
            pltpu.VMEM((total_z * columns, total_y), jnp.bfloat16),
            pltpu.VMEM((total_z, columns, rows), jnp.float32),
            pltpu.SemaphoreType.DMA((components,)),
            pltpu.SemaphoreType.DMA((components,)),
            pltpu.SemaphoreType.DMA((components,)),
            pltpu.SemaphoreType.DMA((components,)),
        ],
        compiler_params=pltpu.CompilerParams(
            collective_id=0, has_side_effects=True, vmem_limit_bytes=48 * 2**20
        ),
    )(inverse_z, high, low, sent)


def turn_body(back_ref, out_ref):
    devices, depth, columns, rows = back_ref.shape[1:]
    for plane in range(depth):
        out_ref[0, plane] = back_ref[0, :, plane].reshape(devices * columns, rows).T


def turn(back):
    components, devices, depth, columns, rows = back.shape
    width = devices * columns
    return pl.pallas_call(
        turn_body,
        grid=(components,),
        in_specs=[pl.BlockSpec((1, devices, depth, columns, rows), lambda v: (v, 0, 0, 0, 0))],
        out_specs=pl.BlockSpec((1, depth, rows, width), lambda v: (v, 0, 0, 0)),
        out_shape=jax.ShapeDtypeStruct((components, depth, rows, width), jnp.float32),
        compiler_params=pltpu.CompilerParams(vmem_limit_bytes=32 * 2**20),
    )(back)


def shards_exchange(adjoint, source, jacobian, inverse_x, inverse_y, inverse_z):
    groups = lax.axis_size("grp")
    lines = lax.axis_size("line")
    padded = padded_2(adjoint, (("grp", 1), ("line", 2)), 2)
    residual = stencil_sum(padded, source, jacobian)
    sent = sweep_x(*split_halves(inverse_x), residual, groups * lines)
    back = middle(inverse_z, *split_halves(inverse_y), sent, groups, lines)
    return turn(back)


def shards(adjoint, source, jacobian, inverse_x, inverse_y, inverse_z):
    devices = lax.axis_size("grp") * lax.axis_size("line")
    whole_tiles = adjoint.shape[2] % 128 == 0 and (adjoint.shape[3] // devices) % 16 == 0
    chosen = shards_exchange if whole_tiles else shards_plain
    return chosen(adjoint, source, jacobian, inverse_x, inverse_y, inverse_z)


def solution(mesh):
    placed = (P(None, "grp", "line", None), P(None, "grp", "line", None), P(), P(), P(), P())
    return jax.shard_map(
        shards, mesh=mesh, in_specs=placed, out_specs=P(None, "grp", "line", None), check_vma=False
    )
```

profile of v0, /device:TPU:11, one launch (start us, length us, event | category | flops | bytes accessed | tf_op | source)
XLA Modules:
  0.0 929.3 jit_solution(405906610164257940)
XLA Ops:
  0.0 10.3 %fusion.14 = (f32[5,2,128,1024]{3,2,1,0:T(8,128)}, f32[5,2,128,1024]{3,2,1,0:T(8,128)}) fusion(f32[5,4,128,1024]{3,2,1,0:T(8,128)} %param.6), kind=kLoop, calls=%fused_computation.39 | loop fusion | bytes 20971520 | tf_op jit(solution)/shard_map/slice | solution.py:18
  10.3 3.1 collective-permute-start.1
  13.4 4.5 collective-permute-start
  18.0 0.7 fusion.19
  18.7 0.7 fusion.18
  19.4 0.7 fusion.17
  20.2 0.7 fusion.16
  20.9 9.0 fusion.15
  29.9 12.2 %subtract_multiply_fusion = f32[5,4,128,1024]{3,2,1,0:T(8,128)} fusion(f32[5,4,128,1023]{3,2,1,0:T(8,128)} %get-tuple-element.15, f32[5,4,128,1023]{3,2,1,0:T(8,128)} %get-tuple-element.14), kind=kLoop, calls=%fused_computation.16 | loop fusion | flops 5242880 | bytes 31436800 | tf_op jit(solution)/shard_map/mul | solution.py:59
  42.1 3.0 fusion.11
  45.0 2.3 fusion.10
  47.3 8.8 fusion.13
  56.2 70.3 %collective-permute-done.1 = f32[5,2,128,1024]{3,2,1,0:T(8,128)} collective-permute-done((f32[5,2,128,1024]{3,2,1,0:T(8,128)}, f32[5,2,128,1024]{3,2,1,0:T(8,128)}, u32[]{:S(2)}, u32[]{:S(2)}) %collective-permute-start.1) | collective-permute-done | bytes 5242912 | tf_op jit(solution)/shard_map/ppermute | solution.py:22
  126.4 8.1 constant_dynamic-update-slice_fusion.3
  134.6 12.1 %constant_dynamic-update-slice_fusion.1 = (f32[5,6,128,1024]{3,2,1,0:T(8,128)}, f32[5,8,128,1024]{3,2,1,0:T(8,128)}, f32[5,6,128,1024]{3,2,1,0:T(8,128)}) fusion(f32[5,4,128,1024]{3,2,1,0:T(8,128)S(1)} %copy-done.5, f32[5,8,128,1024]{3,2,1,0:T(8,128)} %get-tuple-element.19, f32[5,6,128,1024]{3,2,1,0:T(8,128)} %get-tuple-element.18), kind=kLoop, calls=%fused_computation.31 | loop fusion | bytes 41943040
  146.7 93.1 %collective-permute-done = f32[5,2,128,1024]{3,2,1,0:T(8,128)} collective-permute-done((f32[5,2,128,1024]{3,2,1,0:T(8,128)}, f32[5,2,128,1024]{3,2,1,0:T(8,128)}, u32[]{:S(2)}, u32[]{:S(2)}) %collective-permute-start) | collective-permute-done | bytes 5242912 | tf_op jit(solution)/shard_map/ppermute | solution.py:24
  239.8 8.1 constant_dynamic-update-slice_fusion
  247.9 2.0 fusion.12
  249.9 3.5 collective-permute-start.2
  253.4 3.3 collective-permute-start.3
  256.7 14.7 %subtract_multiply_fusion.2 = f32[5,4,128,1024]{3,2,1,0:T(8,128)} fusion(f32[5,6,128,1024]{3,2,1,0:T(8,128)} %get-tuple-element.11, f32[5,6,128,1024]{3,2,1,0:T(8,128)} %get-tuple-element.16), kind=kLoop, calls=%fused_computation.18 | loop fusion | flops 5242880 | bytes 31457280 | tf_op jit(solution)/shard_map/mul | solution.py:59
  271.3 12.5 %subtract_multiply_fusion.1 = f32[5,4,128,1024]{3,2,1,0:T(8,128)} fusion(f32[5,8,2,1024]{3,2,1,0:T(2,128)S(1)} %collective-permute-done.2, f32[5,8,128,1024]{3,2,1,0:T(8,128)} %get-tuple-element.17, f32[5,8,2,1024]{3,2,1,0:T(2,128)S(1)} %collective-permute-done.3), kind=kLoop, calls=%fused_computation.17 | loop fusion | flops 10485760 | bytes 32112640 | tf_op jit(solution)/shard_map/mul | solution.py:59
  283.8 24.7 %add_dynamic-update-slice_fusion.4 = f32[5,4,128,1024]{3,2,1,0:T(8,128)} fusion(f32[5,4,128,1024]{3,2,1,0:T(8,128)} %param.7, f32[5,4,128,1024]{3,2,1,0:T(8,128)} %subtract_multiply_fusion, f32[5,4,128,1024]{3,2,1,0:T(8,128)} %subtract_multiply_fusion.1, f32[5,4,128,1024]{3,2,1,0:T(8,128)} %subtract_multiply_fusion.2, f32[]{:T(128)} %bitcast.14, ...), kind=kLoop, calls=%fused_computation.29 | loop fusion | flops 15728639 | bytes 35651644
  308.5 20.5 %add_dynamic-update-slice_fusion.3 = f32[5,4,128,1024]{3,2,1,0:T(8,128)} fusion(f32[5,4,128,1024]{3,2,1,0:T(8,128)} %add_dynamic-update-slice_fusion.4, f32[5,4,128,1024]{3,2,1,0:T(8,128)} %param.7, f32[5,4,128,1024]{3,2,1,0:T(8,128)S(1)} %bitcast.76, f32[5,4,128,1024]{3,2,1,0:T(8,128)} %subtract_multiply_fusion.1, ...), kind=kLoop, calls=%fused_computation.28 | loop fusion | flops 15728640 | bytes 35659264
  329.0 20.4 %add_dynamic-update-slice_fusion.2 = f32[5,4,128,1024]{3,2,1,0:T(8,128)} fusion(f32[5,4,128,1024]{3,2,1,0:T(8,128)} %add_dynamic-update-slice_fusion.3, f32[5,4,128,1024]{3,2,1,0:T(8,128)} %param.7, f32[5,4,128,1024]{3,2,1,0:T(8,128)S(1)} %bitcast.76, f32[5,4,128,1024]{3,2,1,0:T(8,128)} %subtract_multiply_fusion.1, ...), kind=kLoop, calls=%fused_computation.27 | loop fusion | flops 15728640 | bytes 35659264
  349.4 20.4 %add_dynamic-update-slice_fusion.1 = f32[5,4,128,1024]{3,2,1,0:T(8,128)} fusion(f32[5,4,128,1024]{3,2,1,0:T(8,128)} %add_dynamic-update-slice_fusion.2, f32[5,4,128,1024]{3,2,1,0:T(8,128)} %param.7, f32[5,4,128,1024]{3,2,1,0:T(8,128)S(1)} %bitcast.76, f32[5,4,128,1024]{3,2,1,0:T(8,128)} %subtract_multiply_fusion.1, ...), kind=kLoop, calls=%fused_computation.26 | loop fusion | flops 15728640 | bytes 35659264
  369.8 20.6 %add_dynamic-update-slice_fusion = f32[5,4,128,1024]{3,2,1,0:T(8,128)} fusion(f32[5,4,128,1024]{3,2,1,0:T(8,128)} %add_dynamic-update-slice_fusion.1, f32[5,4,128,1024]{3,2,1,0:T(8,128)} %param.7, f32[5,4,128,1024]{3,2,1,0:T(8,128)S(1)} %bitcast.76, f32[5,4,128,1024]{3,2,1,0:T(8,128)} %subtract_multiply_fusion.1, ...), kind=kLoop, calls=%fused_computation.25 | loop fusion | flops 15728640 | bytes 35659264 | tf_op jit(solution)/shard_map/stack | solution.py:70
  390.4 51.4 %fusion.4.field_ref = f32[5,4,128,1024]{3,2,1,0:T(8,128)} fusion(f32[5,4,128,1024]{3,2,1,0:T(8,128)} %add_dynamic-update-slice_fusion, f32[5,8,128,1024]{3,2,1,0:T(8,128)} %get-tuple-element.17, f32[5,8,2,1024]{3,2,1,0:T(2,128)S(1)} %collective-permute-done.3, f32[5,8,2,1024]{3,2,1,0:T(2,128)S(1)} %collective-permute-done.2, ...), kind=kLoop, calls=%fused_computation.5 | loop fusion | flops 70778880 | bytes 136908800 | tf_op jit(solution)/shard_map/sub | solution.py:70
  441.8 20.3 %shard_map.64.sent_ref = f32[5,32,4,32,128]{4,3,2,1,0:T(8,128)} custom-call(bf16[1024,1024]{1,0:T(8,128)(2,1)S(1)} %copy-done.3, bf16[1024,1024]{1,0:T(8,128)(2,1)S(1)} %copy-done.2, f32[5,4,128,1024]{3,2,1,0:T(8,128)} %fusion.4.field_ref), custom_call_target="tpu_custom_call" | custom-call | tf_op jit(solution)/shard_map/pallas_call | solution.py:138
  462.2 457.3 %shard_map.65.back_ref = f32[5,32,4,32,128]{4,3,2,1,0:T(8,128)} custom-call(f32[16,16]{1,0:T(8,128)S(1)} %copy-done.4, bf16[1024,1024]{1,0:T(8,128)(2,1)S(1)} %copy-done.1, bf16[1024,1024]{1,0:T(8,128)(2,1)S(1)} %get-tuple-element.22.low_ref, f32[5,32,4,32,128]{4,3,2,1,0:T(8,128)} %shard_map.64.sent_ref), custom_call_target="tpu_custom_call" | custom-call | tf_op jit(solution)/shard_map/pallas_call | solution.py:262
  919.5 4.0 copy-done
  923.5 5.8 shard_map.66
  (26 shorter events, 0.1 us)
Async XLA Ops:
  0.0 18.0 %copy-start.8 = (f32[3,5,5]{2,0,1:T(4,128)S(1)}, f32[3,5,5]{2,0,1:T(4,128)}, u32[]{:S(2)}) copy-start(f32[3,5,5]{2,0,1:T(4,128)} %param.8) | copy-start | bytes 904
  0.0 20.9 %copy-start.5 = (f32[5,4,128,1024]{3,2,1,0:T(8,128)S(1)}, f32[5,4,128,1024]{3,2,1,0:T(8,128)}, u32[]{:S(2)}) copy-start(f32[5,4,128,1024]{3,2,1,0:T(8,128)} %param.6) | copy-start | bytes 31457284
  10.3 116.1 %collective-permute-start.1 = (f32[5,2,128,1024]{3,2,1,0:T(8,128)}, f32[5,2,128,1024]{3,2,1,0:T(8,128)}, u32[]{:S(2)}, u32[]{:S(2)}) collective-permute-start(f32[5,2,128,1024]{3,2,1,0:T(8,128)} %get-tuple-element.13), channel_id=1, source_target_pairs={{0,8},{8,16},{16,24},{1,9},{9,17},{17,25},{2,10},{10,18},{18,26},{... | collective-permute-start | bytes 15728648 | tf_op jit(solution)/shard_map/ppermute | solution.py:22
  13.4 226.3 %collective-permute-start = (f32[5,2,128,1024]{3,2,1,0:T(8,128)}, f32[5,2,128,1024]{3,2,1,0:T(8,128)}, u32[]{:S(2)}, u32[]{:S(2)}) collective-permute-start(f32[5,2,128,1024]{3,2,1,0:T(8,128)} %get-tuple-element.12), channel_id=1, source_target_pairs={{8,0},{16,8},{24,16},{9,1},{17,9},{25,17},{10,2},{18,10},{26,18},{... | collective-permute-start | bytes 15728648 | tf_op jit(solution)/shard_map/ppermute | solution.py:24
  29.9 12.2 %copy-start.6 = (f32[1024,1024]{1,0:T(8,128)S(1)}, f32[1024,1024]{1,0:T(8,128)}, u32[]{:S(2)}) copy-start(f32[1024,1024]{1,0:T(8,128)} %param.9) | copy-start | bytes 12582916
  42.1 3.0 copy-start.7
  249.9 21.4 %collective-permute-start.2 = (f32[5,8,2,1024]{3,2,1,0:T(2,128)S(1)}, f32[5,8,2,1024]{3,2,1,0:T(2,128)S(1)}, u32[]{:S(2)}, u32[]{:S(2)}) collective-permute-start(f32[5,8,2,1024]{3,2,1,0:T(2,128)S(1)} %get-tuple-element.6), channel_id=1, source_target_pairs={{1,0},{2,1},{3,2},{4,3},{5,4},{6,5},{7,6},{9,8},{10,9},{11,10},{12... | collective-permute-start | bytes 983048 | tf_op jit(solution)/shard_map/ppermute | solution.py:24
  253.4 18.0 %collective-permute-start.3 = (f32[5,8,2,1024]{3,2,1,0:T(2,128)S(1)}, f32[5,8,2,1024]{3,2,1,0:T(2,128)S(1)}, u32[]{:S(2)}, u32[]{:S(2)}) collective-permute-start(f32[5,8,2,1024]{3,2,1,0:T(2,128)S(1)} %get-tuple-element.5), channel_id=1, source_target_pairs={{0,1},{1,2},{2,3},{3,4},{4,5},{5,6},{6,7},{8,9},{9,10},{10,11},{11... | collective-permute-start | bytes 983048 | tf_op jit(solution)/shard_map/ppermute | solution.py:22
  283.8 24.7 %slice-start = ((s8[10485760]{0:T(1024)(128)(4,1)}), s8[4194304]{0:T(1024)(128)(4,1)S(1)}, s32[]{:S(2)}) async-start(s8[10485760]{0:T(1024)(128)(4,1)} %bitcast.75), calls=%async_computation | async-start | bytes 8388608
  283.8 24.7 %slice-start.1 = ((s8[10485760]{0:T(1024)(128)(4,1)}), s8[4194304]{0:T(1024)(128)(4,1)S(1)}, s32[]{:S(2)}) async-start(s8[10485760]{0:T(1024)(128)(4,1)} %bitcast.75), calls=%async_computation.1 | async-start | bytes 8388608
  283.8 24.7 %slice-start.2 = ((s8[10485760]{0:T(1024)(128)(4,1)}), s8[2097152]{0:T(1024)(128)(4,1)S(1)}, s32[]{:S(2)}) async-start(s8[10485760]{0:T(1024)(128)(4,1)} %bitcast.75), calls=%async_computation.2 | async-start | bytes 4194304
  390.4 51.4 %copy-start.2 = (bf16[1024,1024]{1,0:T(8,128)(2,1)S(1)}, bf16[1024,1024]{1,0:T(8,128)(2,1)}, u32[]{:S(2)}) copy-start(bf16[1024,1024]{1,0:T(8,128)(2,1)} %get-tuple-element.20.low_ref) | copy-start | bytes 6291460
  390.4 51.4 %copy-start.3 = (bf16[1024,1024]{1,0:T(8,128)(2,1)S(1)}, bf16[1024,1024]{1,0:T(8,128)(2,1)}, u32[]{:S(2)}) copy-start(bf16[1024,1024]{1,0:T(8,128)(2,1)} %get-tuple-element.21.high_ref) | copy-start | bytes 6291460
  441.8 20.3 %copy-start.1 = (bf16[1024,1024]{1,0:T(8,128)(2,1)S(1)}, bf16[1024,1024]{1,0:T(8,128)(2,1)}, u32[]{:S(2)}) copy-start(bf16[1024,1024]{1,0:T(8,128)(2,1)} %get-tuple-element.23.high_ref) | copy-start | bytes 6291460
  441.8 20.3 %copy-start.4 = (f32[16,16]{1,0:T(8,128)S(1)}, f32[16,16]{1,0:T(8,128)}, u32[]{:S(2)}) copy-start(f32[16,16]{1,0:T(8,128)} %z_ref.1) | copy-start | bytes 3076
  919.5 4.0 copy-start
where the time goes:
time: 930 us; the launch traced here: 929 us
  Pallas kernels  483 us (52%)
  other arithmetic  203 us (22%)
  waiting for transfers between devices  163 us (18%)
  local copies, waits for them, and re-layouts  65.4 us (7%)
  starting transfers between devices  14.4 us (2%)
    pallas_call x1, Pallas kernels, middle(): pl.pallas_call(functools.partial(middle_body, groups, lines), in_specs=[p...  457 us
    ppermute x2, waiting for transfers between devices, padded_2(): lax.ppermute(head, axis, [((i + 1) % count, i) for i in range(ends)])  93.1 us
    unnamed x5, other arithmetic  86 us
    ppermute x2, waiting for transfers between devices, padded_2(): lax.ppermute(tail, axis, [(i, (i + 1) % count) for i in range(ends)])  70.3 us
    sub x1, other arithmetic, stencil_sum(): return jnp.stack(outputs, axis=0) - dissipation * damping  51.4 us
    mul x3, other arithmetic, stencil_sum(): centrals.append(0.5 * (forward - backward))  39.3 us
    unnamed x26, local copies, waits for them, and re-layouts  24.2 us
    another operation x1, other arithmetic, stencil_sum(): return jnp.stack(outputs, axis=0) - dissipation * damping  20.6 us
  transfers between devices with their start and end apart: 4, of which 2 were waited for; matrix products, arithmetic and copies ran while one was open for 8% of the time, Pallas kernels for 0%

commit v1 on v0

--- a/solution.py
+++ b/solution.py
@@ -123,30 +123,139 @@
     return one(left[0], right[0]) + (one(left[0], right[1]) + one(left[1], right[0]))
 
 
-def sweep_x_body(high_ref, low_ref, field_ref, out_ref):
-    depth, rows, width = field_ref.shape[1:]
-    field = halves(field_ref[0].reshape(depth * rows, width))
-    swept = product((high_ref[...], low_ref[...]), field)
+def shift_x(field, offset, place):
+    width = field.shape[-1]
+    moved = pltpu.roll(field, (-offset) % width, axis=1)
+    inside = place < width - offset if offset > 0 else place >= -offset
+    return jnp.where(inside, moved, 0.0)
+
+
+def residual_sweep_body(
+    jacobian_ref, high_ref, low_ref, source_ref, cells_ref, below_ref, above_ref, before_ref, after_ref,
+    out_ref, padded, residual, sems,
+):
+    v = pl.program_id(0)
+    components = cells_ref.shape[0]
+    depth, rows, width = source_ref.shape[1:]
+
+    @pl.when(v == 0)
+    def _():
+        inner = pl.ds(2, depth)
+        middle_rows = pl.ds(8, rows)
+        copies = [
+            pltpu.make_async_copy(cells_ref, padded.at[:, inner, middle_rows], sems.at[0]),
+            pltpu.make_async_copy(below_ref, padded.at[:, pl.ds(0, 2), middle_rows], sems.at[1]),
+            pltpu.make_async_copy(above_ref, padded.at[:, pl.ds(depth + 2, 2), middle_rows], sems.at[2]),
+            pltpu.make_async_copy(before_ref, padded.at[:, inner, pl.ds(0, 8)], sems.at[3]),
+            pltpu.make_async_copy(after_ref, padded.at[:, inner, pl.ds(rows + 8, 8)], sems.at[4]),
+        ]
+        for copy in copies:
+            copy.start()
+        for copy in copies:
+            copy.wait()
+
+    place = lax.broadcasted_iota(jnp.int32, (8, width), 1)
+    row = lax.broadcasted_iota(jnp.int32, (8, width), 0)
+    factors = [[0.5 * jacobian_ref[d, w, v] for w in range(components)] for d in range(3)]
+
+    def plane(z):
+        def read(w, dz, start):
+            return padded[w, z + 2 + dz, pl.ds(start, 8), :]
+
+        def along(start):
+            total = factors[1][0] * read(0, 0, start)
+            for w in range(1, components):
+                total = total + factors[1][w] * read(w, 0, start)
+            return total
+
+        def tile(t, carry):
+            behind, here = carry
+            start = pl.multiple_of(t * 8, 8)
+            at = pl.multiple_of(t * 8 + 8, 8)
+            after = pl.multiple_of(t * 8 + 16, 8)
+            ahead = along(after)
+            total = source_ref[0, z, pl.ds(start, 8), :]
+            across = factors[2][0] * read(0, 0, at)
+            for w in range(1, components):
+                across = across + factors[2][w] * read(w, 0, at)
+            for w in range(components):
+                total = total + factors[0][w] * (read(w, 1, at) - read(w, -1, at))
+            centre, last, coming = read(v, 0, at), read(v, 0, start), read(v, 0, after)
+            scale = 4.0 * dissipation
+            total = total + scale * (read(v, 1, at) + read(v, -1, at))
+            scaled = scale * centre
+            forward = jnp.where(row == 0, scale * coming + ahead, scaled + here)
+            backward = jnp.where(row == 7, scale * last - behind, scaled - here)
+            total = total + pltpu.roll(forward, 7, axis=0) + pltpu.roll(backward, 1, axis=0)
+            total = total + shift_x(scaled + across, 1, place) + shift_x(scaled - across, -1, place)
+            far = read(v, 2, at) + read(v, -2, at)
+            far = far + pltpu.roll(jnp.where(row < 2, coming, centre), 6, axis=0)
+            far = far + pltpu.roll(jnp.where(row >= 6, last, centre), 2, axis=0)
+            far = far + shift_x(centre, 2, place) + shift_x(centre, -2, place)
+            total = total - dissipation * (far + 18.0 * centre)
+            residual[pl.ds(pl.multiple_of(z * rows + start, 8), 8), :] = total
+            return here, ahead
+
+        lax.fori_loop(0, rows // 8, tile, (along(0), along(8)))
+
+    for z in range(depth):
+        plane(z)
+    swept = product((high_ref[...], low_ref[...]), halves(residual[...]))
     for plane in range(depth):
         part = swept[:, plane * rows : (plane + 1) * rows]
         out_ref[0, :, plane] = part.reshape(out_ref.shape[1], out_ref.shape[3], rows)
 
 
-def sweep_x(high, low, residual, devices):
-    components, depth, rows, width = residual.shape
+def residual_sweep(jacobian, high, low, source, cells, rims, devices):
+    components, depth, rows, width = source.shape
     columns = width // devices
+    once = pl.Buffered(1)
     return pl.pallas_call(
-        sweep_x_body,
+        residual_sweep_body,
         grid=(components,),
         in_specs=[
-            pl.BlockSpec((width, width), lambda v: (0, 0)),
-            pl.BlockSpec((width, width), lambda v: (0, 0)),
+            pl.BlockSpec(memory_space=pltpu.SMEM),
+            pl.BlockSpec((width, width), lambda v: (0, 0), pipeline_mode=once),
+            pl.BlockSpec((width, width), lambda v: (0, 0), pipeline_mode=once),
             pl.BlockSpec((1, depth, rows, width), lambda v: (v, 0, 0, 0)),
-        ],
+        ]
+        + [pl.BlockSpec(memory_space=pl.ANY)] * 5,
         out_specs=pl.BlockSpec((1, devices, depth, columns, rows), lambda v: (v, 0, 0, 0, 0)),
         out_shape=jax.ShapeDtypeStruct((components, devices, depth, columns, rows), jnp.float32),
-        compiler_params=pltpu.CompilerParams(vmem_limit_bytes=48 * 2**20),
-    )(high, low, residual)
+        scratch_shapes=[
+            pltpu.VMEM((components, depth + 4, rows + 16, width), jnp.float32),
+            pltpu.VMEM((depth * rows, width), jnp.float32),
+            pltpu.SemaphoreType.DMA((5,)),
+        ],
+        compiler_params=pltpu.CompilerParams(vmem_limit_bytes=56 * 2**20),
+    )(jacobian, high, low, source, cells, *rims)
+
+
+def rims_of(cells):
+    rims = []
+    for axis, dim, width in (("grp", 1, 2), ("line", 2, 8)):
+        count = lax.axis_size(axis)
+        size = cells.shape[dim]
+        head = lax.slice_in_dim(cells, 0, width, axis=dim)
+        tail = lax.slice_in_dim(cells, size - width, size, axis=dim)
+        if axis == "grp" and count == 4:
+            rims.append(relayed(tail, ((0, 1), (2, 3)), (1, 3, 2)))
+            rims.append(relayed(head, ((1, 0), (3, 2)), (2, 0, 1)))
+        else:
+            rims.append(lax.ppermute(tail, axis, [(i, i + 1) for i in range(count - 1)]))
+            rims.append(lax.ppermute(head, axis, [(i + 1, i) for i in range(count - 1)]))
+    return rims
+
+
+def relayed(rim, near, route):
+    first, corner, last = route
+    half = rim.shape[-1] // 2
+    direct = lax.ppermute(rim[..., :half], "grp", [*near, (first, last)])
+    side = lax.ppermute(rim[..., half:], "grp", [(first, corner)])
+    rest = lax.ppermute(rim[..., half:], "grp", list(near))
+    side = lax.ppermute(side, "grp", [(corner, last)])
+    mine = lax.axis_index("grp") == last
+    return jnp.concatenate([direct, jnp.where(mine, side, rest)], axis=-1)
 
 
 def middle_body(
@@ -308,9 +417,10 @@
 def shards_exchange(adjoint, source, jacobian, inverse_x, inverse_y, inverse_z):
     groups = lax.axis_size("grp")
     lines = lax.axis_size("line")
-    padded = padded_2(adjoint, (("grp", 1), ("line", 2)), 2)
-    residual = stencil_sum(padded, source, jacobian)
-    sent = sweep_x(*split_halves(inverse_x), residual, groups * lines)
+    rims = rims_of(adjoint)
+    sent = residual_sweep(
+        jacobian, *split_halves(inverse_x), source, adjoint, rims, groups * lines
+    )
     back = middle(inverse_z, *split_halves(inverse_y), sent, groups, lines)
     return turn(back)
 

time: 930 us -> 780 us (0.84)
  other arithmetic: 203 us -> 20.3 us
  starting transfers between devices: 14.4 us -> 81.4 us
  local copies, waits for them, and re-layouts: 65.4 us -> 15.4 us
  Pallas kernels: 483 us -> 531 us
  waiting for transfers between devices: 163 us -> 130 us
    unnamed x5 -> x0, other arithmetic: 86 us -> none
    ppermute x4 -> x10, starting transfers between devices: 14.4 us -> 81.4 us  [the longest x2 59.2 us: relayed(): direct = lax.ppermute(rim[..., :half], 'grp', [*near, (first, last)])]
    sub x1 -> x0, other arithmetic: 51.4 us -> none  [stencil_sum(): return jnp.stack(outputs, axis=0) - dissipation * damping]
    pallas_call x1, Pallas kernels: 20.3 us -> 63.7 us  [residual_sweep(): pl.pallas_call(residual_sweep_body, grid=(components,), in_specs=[pl.Bloc...]
    mul x3 -> x0, other arithmetic: 39.3 us -> none  [stencil_sum(): centrals.append(0.5 * (forward - backward))]
    ppermute x4 -> x10, waiting for transfers between devices: 163 us -> 130 us  [the longest x2 53.8 us: relayed(): direct = lax.ppermute(rim[..., :half], 'grp', [*near, (first, last)])]
    slice x8 -> x2, local copies, waits for them, and re-layouts: 33 us -> 9.75 us  [the longest x1 8.33 us: relayed(): direct = lax.ppermute(rim[..., :half], 'grp', [*near, (first, last)])]
    another operation x1 -> x0, other arithmetic: 20.6 us -> none  [stencil_sum(): return jnp.stack(outputs, axis=0) - dissipation * damping]
  transfers between devices with their start and end apart: 4 -> 10, of which waited for: 2 -> 3; matrix products, arithmetic and copies ran while one was open for 8% -> 3% of each run, Pallas kernels for 0% -> 0%
where the time goes in v1:
time: 780 us; the launch traced here: 779 us
  Pallas kernels  531 us (68%)
  waiting for transfers between devices  130 us (17%)
  starting transfers between devices  81.4 us (10%)
  other arithmetic  20.3 us (3%)
  local copies, waits for them, and re-layouts  15.4 us (2%)
    pallas_call x1, Pallas kernels, middle(): pl.pallas_call(functools.partial(middle_body, groups, lines), in_specs=[p...  462 us
    pallas_call x1, Pallas kernels, residual_sweep(): pl.pallas_call(residual_sweep_body, grid=(components,), in_specs=[pl.Bloc...  63.7 us
    ppermute x2, starting transfers between devices, relayed(): direct = lax.ppermute(rim[..., :half], 'grp', [*near, (first, last)])  59.2 us
    ppermute x2, waiting for transfers between devices, relayed(): direct = lax.ppermute(rim[..., :half], 'grp', [*near, (first, last)])  53.8 us
    ppermute x2, waiting for transfers between devices, relayed(): rest = lax.ppermute(rim[..., half:], 'grp', list(near))  40.1 us
    ppermute x2, waiting for transfers between devices, relayed(): side = lax.ppermute(side, 'grp', [(corner, last)])  36.4 us
  transfers between devices with their start and end apart: 10, of which 3 were waited for; matrix products, arithmetic and copies ran while one was open for 3% of the time, Pallas kernels for 0%

profile of v1, /device:TPU:11, one launch (start us, length us, event | category | flops | bytes accessed | tf_op | source)
XLA Modules:
  0.0 779.1 jit_solution(11946859838831970853)
XLA Ops:
  0.0 8.3 %fusion.3 = (f32[5,2,128,512]{3,2,1,0:T(8,128)}, f32[5,2,128,512]{3,2,1,0:T(8,128)S(1)}, f32[5,2,128,512]{3,2,1,0:T(8,128)}, f32[5,2,128,512]{3,2,1,0:T(8,128)S(1)}) fusion(f32[5,4,128,1024]{3,2,1,0:T(8,128)} %cells_ref.1), kind=kLoop, calls=%fused_computation.11 | loop fusion | bytes 20971520 | tf_op jit(solution)/shard_map/slice | solution.py:253
  8.3 2.2 collective-permute-start.5
  10.5 4.7 collective-permute-start.1
  15.2 1.4 collective-permute-start.7
  16.7 0.0 collective-permute-done.5
  16.7 1.3 collective-permute-start.6
  18.0 55.0 %collective-permute-start.4 = (f32[5,2,128,512]{3,2,1,0:T(8,128)}, f32[5,2,128,512]{3,2,1,0:T(8,128)}, u32[]{:S(2)}, u32[]{:S(2)}) collective-permute-start(f32[5,2,128,512]{3,2,1,0:T(8,128)} %get-tuple-element.7), channel_id=1, source_target_pairs={{8,0},{24,16},{16,8},{9,1},{25,17},{17,9},{10,2},{26,18},{18,10},{... | collective-permute-start | bytes 7864328 | tf_op jit(solution)/shard_map/ppermute | solution.py:253
  73.0 1.3 collective-permute-start.3
  74.3 2.3 collective-permute-start.2
  76.6 0.0 collective-permute-done.7
  76.6 4.2 collective-permute-start
  80.8 0.6 copy.7.jacobian_ref
  81.4 1.4 fusion.2
  82.9 0.0 copy-start.2
  82.9 5.3 fusion.1
  88.2 0.9 fusion
  89.1 36.4 %collective-permute-done.6 = f32[5,2,128,512]{3,2,1,0:T(8,128)} collective-permute-done((f32[5,2,128,512]{3,2,1,0:T(8,128)}, f32[5,2,128,512]{3,2,1,0:T(8,128)}, u32[]{:S(2)}, u32[]{:S(2)}) %collective-permute-start.6) | collective-permute-done | bytes 2621472 | tf_op jit(solution)/shard_map/ppermute | solution.py:256
  125.5 7.1 collective-permute-start.8
  132.6 2.4 broadcast_select_fusion
  135.0 0.0 collective-permute-done.4
  135.0 1.9 collective-permute-start.9
  136.9 4.7 pad_maximum_fusion.1.above_ref
  141.6 40.1 %collective-permute-done.3 = f32[5,2,128,512]{3,2,1,0:T(8,128)} collective-permute-done((f32[5,2,128,512]{3,2,1,0:T(8,128)}, f32[5,2,128,512]{3,2,1,0:T(8,128)}, u32[]{:S(2)}, u32[]{:S(2)}) %collective-permute-start.3) | collective-permute-done | bytes 2621472 | tf_op jit(solution)/shard_map/ppermute | solution.py:255
  181.7 2.4 broadcast_select_fusion.1
  184.1 53.8 %collective-permute-done = f32[5,2,128,512]{3,2,1,0:T(8,128)} collective-permute-done((f32[5,2,128,512]{3,2,1,0:T(8,128)S(1)}, f32[5,2,128,512]{3,2,1,0:T(8,128)}, u32[]{:S(2)}, u32[]{:S(2)}) %collective-permute-start) | collective-permute-done | bytes 2621472 | tf_op jit(solution)/shard_map/ppermute | solution.py:253
  237.9 4.7 pad_maximum_fusion.below_ref
  242.6 0.8 copy-done.6
  243.4 0.2 copy-done.5
  243.7 63.7 %shard_map.64.sent_ref = f32[5,32,4,32,128]{4,3,2,1,0:T(8,128)} custom-call(f32[3,5,5]{2,1,0:T(8,128)} %copy.7.jacobian_ref, bf16[1024,1024]{1,0:T(8,128)(2,1)} %get-tuple-element.12.high_ref, bf16[1024,1024]{1,0:T(8,128)(2,1)} %get-tuple-element.11.low_ref, f32[5,4,128,1024]{3,2,1,0:T(8,128)} %source_ref.1, f32[5,4,128,1024]{3,2,1,0:T(8,128)} %cells_ref.1, ...), custom_call_target="tpu_custom_call" | custom-call | tf_op jit(solution)/shard_map/pallas_call | solution.py:213
  307.3 462.0 %shard_map.65.back_ref = f32[5,32,4,32,128]{4,3,2,1,0:T(8,128)} custom-call(f32[16,16]{1,0:T(8,128)S(1)} %copy-done.1, bf16[1024,1024]{1,0:T(8,128)(2,1)S(1)} %get-tuple-element.14.high_ref, bf16[1024,1024]{1,0:T(8,128)(2,1)S(1)} %get-tuple-element.13.low_ref, f32[5,32,4,32,128]{4,3,2,1,0:T(8,128)} %shard_map.64.sent_ref), custom_call_target="tpu_custom_call" | custom-call | tf_op jit(solution)/shard_map/pallas_call | solution.py:371
  769.4 4.0 copy-done
  773.4 5.8 shard_map.66
  (16 shorter events, 0.0 us)
Async XLA Ops:
  0.0 80.8 %copy-start.7 = (f32[3,5,5]{2,0,1:T(4,128)S(1)}, f32[3,5,5]{2,0,1:T(4,128)}, u32[]{:S(2)}) copy-start(f32[3,5,5]{2,0,1:T(4,128)} %param.8) | copy-start | bytes 904
  8.3 8.3 %collective-permute-start.5 = (f32[5,2,128,512]{3,2,1,0:T(8,128)S(1)}, f32[5,2,128,512]{3,2,1,0:T(8,128)}, u32[]{:S(2)}, u32[]{:S(2)}) collective-permute-start(f32[5,2,128,512]{3,2,1,0:T(8,128)S(1)} %get-tuple-element.8), channel_id=1, source_target_pairs={{16,0},{17,1},{18,2},{19,3},{20,4},{21,5},{22,6},{23,7}} | collective-permute-start | bytes 7864328 | tf_op jit(solution)/shard_map/ppermute | solution.py:254
  10.5 63.8 %collective-permute-start.1 = (f32[5,2,128,512]{3,2,1,0:T(8,128)}, f32[5,2,128,512]{3,2,1,0:T(8,128)}, u32[]{:S(2)}, u32[]{:S(2)}) collective-permute-start(f32[5,2,128,512]{3,2,1,0:T(8,128)} %get-tuple-element.9), channel_id=1, source_target_pairs={{8,24},{9,25},{10,26},{11,27},{12,28},{13,29},{14,30},{15,31}} | collective-permute-start | bytes 7864328 | tf_op jit(solution)/shard_map/ppermute | solution.py:254
  15.2 61.4 %collective-permute-start.7 = (f32[5,2,128,512]{3,2,1,0:T(8,128)S(1)}, f32[5,2,128,512]{3,2,1,0:T(8,128)S(1)}, u32[]{:S(2)}, u32[]{:S(2)}) collective-permute-start(f32[5,2,128,512]{3,2,1,0:T(8,128)S(1)} %get-tuple-element.8), channel_id=1, source_target_pairs={{8,0},{24,16},{9,1},{25,17},{10,2},{26,18},{11,3},{27,19},{12,4},{... | collective-permute-start | bytes 7864328 | tf_op jit(solution)/shard_map/ppermute | solution.py:255
  16.7 108.8 %collective-permute-start.6 = (f32[5,2,128,512]{3,2,1,0:T(8,128)}, f32[5,2,128,512]{3,2,1,0:T(8,128)}, u32[]{:S(2)}, u32[]{:S(2)}) collective-permute-start(f32[5,2,128,512]{3,2,1,0:T(8,128)} %collective-permute-done.5), channel_id=1, source_target_pairs={{0,8},{1,9},{2,10},{3,11},{4,12},{5,13},{6,14},{7,15}} | collective-permute-start | bytes 7864328 | tf_op jit(solution)/shard_map/ppermute | solution.py:256
  18.0 117.0 %collective-permute-start.4 = (f32[5,2,128,512]{3,2,1,0:T(8,128)}, f32[5,2,128,512]{3,2,1,0:T(8,128)}, u32[]{:S(2)}, u32[]{:S(2)}) collective-permute-start(f32[5,2,128,512]{3,2,1,0:T(8,128)} %get-tuple-element.7), channel_id=1, source_target_pairs={{8,0},{24,16},{16,8},{9,1},{25,17},{17,9},{10,2},{26,18},{18,10},{... | collective-permute-start | bytes 7864328 | tf_op jit(solution)/shard_map/ppermute | solution.py:253
  73.0 108.7 %collective-permute-start.3 = (f32[5,2,128,512]{3,2,1,0:T(8,128)}, f32[5,2,128,512]{3,2,1,0:T(8,128)}, u32[]{:S(2)}, u32[]{:S(2)}) collective-permute-start(f32[5,2,128,512]{3,2,1,0:T(8,128)} %get-tuple-element.9), channel_id=1, source_target_pairs={{0,8},{16,24},{1,9},{17,25},{2,10},{18,26},{3,11},{19,27},{4,12},{... | collective-permute-start | bytes 7864328 | tf_op jit(solution)/shard_map/ppermute | solution.py:255
  74.3 107.4 %collective-permute-start.2 = (f32[5,2,128,512]{3,2,1,0:T(8,128)}, f32[5,2,128,512]{3,2,1,0:T(8,128)}, u32[]{:S(2)}, u32[]{:S(2)}) collective-permute-start(f32[5,2,128,512]{3,2,1,0:T(8,128)} %collective-permute-done.1), channel_id=1, source_target_pairs={{24,16},{25,17},{26,18},{27,19},{28,20},{29,21},{30,22},{31,23}} | collective-permute-start | bytes 7864328 | tf_op jit(solution)/shard_map/ppermute | solution.py:256
  76.6 4.2 copy-start.3
  76.6 161.3 %collective-permute-start = (f32[5,2,128,512]{3,2,1,0:T(8,128)S(1)}, f32[5,2,128,512]{3,2,1,0:T(8,128)}, u32[]{:S(2)}, u32[]{:S(2)}) collective-permute-start(f32[5,2,128,512]{3,2,1,0:T(8,128)S(1)} %get-tuple-element.10), channel_id=1, source_target_pairs={{0,8},{16,24},{8,16},{1,9},{17,25},{9,17},{2,10},{18,26},{10,18},{... | collective-permute-start | bytes 7864328 | tf_op jit(solution)/shard_map/ppermute | solution.py:253
  82.9 5.3 copy-start.2
  88.2 44.4 %copy-start.4 = (f32[5,2,128,512]{3,2,1,0:T(8,128)S(1)}, f32[5,2,128,512]{3,2,1,0:T(8,128)}, u32[]{:S(2)}) copy-start(f32[5,2,128,512]{3,2,1,0:T(8,128)} %copy-done.3) | copy-start | bytes 7864324
  125.5 117.1 %collective-permute-start.8 = (f32[5,4,8,1024]{3,2,1,0:T(8,128)S(1)}, f32[5,4,8,1024]{3,2,1,0:T(8,128)S(1)}, u32[]{:S(2)}, u32[]{:S(2)}) collective-permute-start(f32[5,4,8,1024]{3,2,1,0:T(8,128)S(1)} %get-tuple-element.6), channel_id=1, source_target_pairs={{0,1},{1,2},{2,3},{3,4},{4,5},{5,6},{6,7},{8,9},{9,10},{10,11},{11... | collective-permute-start | bytes 1966088 | tf_op jit(solution)/shard_map/ppermute | solution.py:245
  135.0 107.6 %collective-permute-start.9 = (f32[5,4,8,1024]{3,2,1,0:T(8,128)S(1)}, f32[5,4,8,1024]{3,2,1,0:T(8,128)S(1)}, u32[]{:S(2)}, u32[]{:S(2)}) collective-permute-start(f32[5,4,8,1024]{3,2,1,0:T(8,128)S(1)} %get-tuple-element.5), channel_id=1, source_target_pairs={{1,0},{2,1},{3,2},{4,3},{5,4},{6,5},{7,6},{9,8},{10,9},{11,10},{12... | collective-permute-start | bytes 1966088 | tf_op jit(solution)/shard_map/ppermute | solution.py:246
  242.6 1.1 copy-start.5
  242.6 0.8 copy-start.6
  243.6 63.7 %copy-start.1 = (f32[16,16]{1,0:T(8,128)S(1)}, f32[16,16]{1,0:T(8,128)}, u32[]{:S(2)}) copy-start(f32[16,16]{1,0:T(8,128)} %z_ref.1) | copy-start | bytes 3076
  769.4 4.0 copy-start

commit v2 on v1

--- a/solution.py
+++ b/solution.py
@@ -131,23 +131,32 @@
 
 
 def residual_sweep_body(
-    jacobian_ref, high_ref, low_ref, source_ref, cells_ref, below_ref, above_ref, before_ref, after_ref,
-    out_ref, padded, residual, sems,
+    pair, jacobian_ref, high_ref, low_ref, source_ref, first_ref, second_ref, before_ref, after_ref, *rest
+
 ):
+    out_ref, padded, residual, sems = rest[-4:]
     v = pl.program_id(0)
-    components = cells_ref.shape[0]
+    components = first_ref.shape[0]
     depth, rows, width = source_ref.shape[1:]
 
     @pl.when(v == 0)
     def _():
         inner = pl.ds(2, depth)
         middle_rows = pl.ds(8, rows)
+        cut = first_ref.shape[1]
         copies = [
-            pltpu.make_async_copy(cells_ref, padded.at[:, inner, middle_rows], sems.at[0]),
-            pltpu.make_async_copy(below_ref, padded.at[:, pl.ds(0, 2), middle_rows], sems.at[1]),
-            pltpu.make_async_copy(above_ref, padded.at[:, pl.ds(depth + 2, 2), middle_rows], sems.at[2]),
-            pltpu.make_async_copy(before_ref, padded.at[:, inner, pl.ds(0, 8)], sems.at[3]),
-            pltpu.make_async_copy(after_ref, padded.at[:, inner, pl.ds(rows + 8, 8)], sems.at[4]),
+            pltpu.make_async_copy(first_ref, padded.at[:, pl.ds(0, cut), middle_rows], sems.at[0]),
+            pltpu.make_async_copy(
+                second_ref, padded.at[:, pl.ds(cut, depth + 4 - cut), middle_rows], sems.at[1]
+            ),
+            pltpu.make_async_copy(
+                before_ref.at[:, pl.ds(pair * depth, depth)], padded.at[:, inner, pl.ds(0, 8)], sems.at[2]
+            ),
+            pltpu.make_async_copy(
+                after_ref.at[:, pl.ds(pair * depth, depth)],
+                padded.at[:, inner, pl.ds(rows + 8, 8)],
+                sems.at[3],
+            ),
         ]
         for copy in copies:
             copy.start()
@@ -206,67 +215,36 @@
         out_ref[0, :, plane] = part.reshape(out_ref.shape[1], out_ref.shape[3], rows)
 
 
-def residual_sweep(jacobian, high, low, source, cells, rims, devices):
+def residual_sweep(pair, jacobian, high, low, source, parts, ahead, devices):
     components, depth, rows, width = source.shape
+    depth = depth // 2
     columns = width // devices
     once = pl.Buffered(1)
     return pl.pallas_call(
-        residual_sweep_body,
+        functools.partial(residual_sweep_body, pair),
         grid=(components,),
         in_specs=[
             pl.BlockSpec(memory_space=pltpu.SMEM),
             pl.BlockSpec((width, width), lambda v: (0, 0), pipeline_mode=once),
             pl.BlockSpec((width, width), lambda v: (0, 0), pipeline_mode=once),
-            pl.BlockSpec((1, depth, rows, width), lambda v: (v, 0, 0, 0)),
+            pl.BlockSpec((1, depth, rows, width), lambda v: (v, pair, 0, 0)),
         ]
-        + [pl.BlockSpec(memory_space=pl.ANY)] * 5,
+        + [pl.BlockSpec(memory_space=pl.ANY)] * (len(parts) + len(ahead)),
         out_specs=pl.BlockSpec((1, devices, depth, columns, rows), lambda v: (v, 0, 0, 0, 0)),
         out_shape=jax.ShapeDtypeStruct((components, devices, depth, columns, rows), jnp.float32),
         scratch_shapes=[
             pltpu.VMEM((components, depth + 4, rows + 16, width), jnp.float32),
             pltpu.VMEM((depth * rows, width), jnp.float32),
-            pltpu.SemaphoreType.DMA((5,)),
+            pltpu.SemaphoreType.DMA((4,)),
         ],
-        compiler_params=pltpu.CompilerParams(vmem_limit_bytes=56 * 2**20),
-    )(jacobian, high, low, source, cells, *rims)
-
-
-def rims_of(cells):
-    rims = []
-    for axis, dim, width in (("grp", 1, 2), ("line", 2, 8)):
-        count = lax.axis_size(axis)
-        size = cells.shape[dim]
-        head = lax.slice_in_dim(cells, 0, width, axis=dim)
-        tail = lax.slice_in_dim(cells, size - width, size, axis=dim)
-        if axis == "grp" and count == 4:
-            rims.append(relayed(tail, ((0, 1), (2, 3)), (1, 3, 2)))
-            rims.append(relayed(head, ((1, 0), (3, 2)), (2, 0, 1)))
-        else:
-            rims.append(lax.ppermute(tail, axis, [(i, i + 1) for i in range(count - 1)]))
-            rims.append(lax.ppermute(head, axis, [(i + 1, i) for i in range(count - 1)]))
-    return rims
-
-
-def relayed(rim, near, route):
-    first, corner, last = route
-    half = rim.shape[-1] // 2
-    direct = lax.ppermute(rim[..., :half], "grp", [*near, (first, last)])
-    side = lax.ppermute(rim[..., half:], "grp", [(first, corner)])
-    rest = lax.ppermute(rim[..., half:], "grp", list(near))
-    side = lax.ppermute(side, "grp", [(corner, last)])
-    mine = lax.axis_index("grp") == last
-    return jnp.concatenate([direct, jnp.where(mine, side, rest)], axis=-1)
-
-
-def middle_body(
-    groups, lines, z_ref, high_ref, low_ref, sent_ref, back_ref,
-    got, done, field_high, field_low, lined, send_one, recv_one, send_two, recv_two,
-):
-    components, devices, depth, columns, rows = sent_ref.shape
-    total_z = groups * depth
+        compiler_params=pltpu.CompilerParams(vmem_limit_bytes=48 * 2**20),
+    )(jacobian, high, low, source, *parts, *ahead)
+
+
+def meet(groups, lines):
+    devices = groups * lines
     own_g = lax.axis_index("grp")
     own_l = lax.axis_index("line")
-    own = own_g * lines + own_l
 
     def partner(step):
         l = lax.rem(own_l + step // groups, lines)
@@ -282,6 +260,57 @@
 
     lax.fori_loop(1, devices, greet, 0)
     pl.semaphore_wait(barrier, devices - 1)
+    return own_g, own_l, partner
+
+
+def spread_body(groups, lines, sent_ref, got_ref, send_sem, recv_sem):
+    components, devices = sent_ref.shape[:2]
+    own_g, own_l, partner = meet(groups, lines)
+    own = own_g * lines + own_l
+    pltpu.make_async_copy(sent_ref.at[:, own], got_ref.at[:, own], recv_sem).start()
+
+    def one(step, c):
+        g, l = partner(step)
+        pltpu.make_async_remote_copy(
+            src_ref=sent_ref.at[:, g * lines + l],
+            dst_ref=got_ref.at[:, own],
+            send_sem=send_sem,
+            recv_sem=recv_sem,
+            device_id=(g, l),
+            device_id_type=MESH,
+        ).start()
+        return c
+
+    lax.fori_loop(1, devices, one, 0)
+    others = pl.ds(0, devices - 1)
+    pltpu.make_async_copy(sent_ref.at[:, others], sent_ref.at[:, others], send_sem).wait()
+    pltpu.make_async_copy(got_ref, got_ref, recv_sem).wait()
+
+
+def spread(sent, groups, lines):
+    return pl.pallas_call(
+        functools.partial(spread_body, groups, lines),
+        in_specs=[pl.BlockSpec(memory_space=pl.ANY)],
+        out_specs=pl.BlockSpec(memory_space=pl.ANY),
+        out_shape=jax.ShapeDtypeStruct(sent.shape, jnp.float32),
+        scratch_shapes=[pltpu.SemaphoreType.DMA, pltpu.SemaphoreType.DMA],
+        cost_estimate=pl.CostEstimate(
+            flops=10**11, bytes_accessed=2 * sent.size * 4, transcendentals=0
+        ),
+        compiler_params=pltpu.CompilerParams(collective_id=1, has_side_effects=True),
+    )(sent)
+
+
+def middle_body(
+    groups, lines, z_ref, high_ref, low_ref, early_ref, sent_ref, back_ref,
+    early, got, done, field_high, field_low, lined, early_sem, send_one, recv_one, send_two, recv_two,
+):
+    components, devices, depth, columns, rows = sent_ref.shape
+    total_z = groups * 2 * depth
+    own_g, own_l, partner = meet(groups, lines)
+    own = own_g * lines + own_l
+    fetch = pltpu.make_async_copy(early_ref, early, early_sem)
+    fetch.start()
 
     def first(v, carry):
         pltpu.make_async_copy(sent_ref.at[v, own], got.at[v, own], recv_one.at[v]).start()
@@ -302,16 +331,20 @@
         return carry
 
     lax.fori_loop(0, components, first, 0)
+    fetch.wait()
 
     def solve(v, carry):
         pltpu.make_async_copy(got.at[v], got.at[v], recv_one.at[v]).wait()
         for g in range(groups):
-            block = jnp.concatenate(
-                [got[v, g * lines + l].reshape(depth * columns, rows) for l in range(lines)], axis=-1
-            )
-            high, low = halves(block)
-            field_high[pl.ds(g * depth * columns, depth * columns), :] = high
-            field_low[pl.ds(g * depth * columns, depth * columns), :] = low
+            for place, half in enumerate((early, got)):
+                block = jnp.concatenate(
+                    [half[v, g * lines + l].reshape(depth * columns, rows) for l in range(lines)],
+                    axis=-1,
+                )
+                high, low = halves(block)
+                at = pl.ds((2 * g + place) * depth * columns, depth * columns)
+                field_high[at, :] = high
+                field_low[at, :] = low
 
         def line(i, c):
             l = lax.rem(own_l + i, lines)
@@ -324,7 +357,7 @@
                 total = z_ref[q, 0] * lined[0]
                 for z in range(1, total_z):
                     total = total + z_ref[q, z] * lined[z]
-                done[v, (q // depth) * lines + l, q % depth] = total
+                done[v, (q // (2 * depth)) * lines + l, q % (2 * depth)] = total
 
             def send(j, cc):
                 g = lax.rem(own_g + j, groups)
@@ -364,10 +397,11 @@
     lax.fori_loop(0, components, finish, 0)
 
 
-def middle(inverse_z, high, low, sent, groups, lines):
+def middle(inverse_z, high, low, early, sent, groups, lines):
     components, devices, depth, columns, rows = sent.shape
     total_y = high.shape[0]
-    total_z = groups * depth
+    total_z = groups * 2 * depth
+    whole = (components, devices, 2 * depth, columns, rows)
     return pl.pallas_call(
         functools.partial(middle_body, groups, lines),
         in_specs=[
@@ -375,15 +409,18 @@
             pl.BlockSpec(memory_space=pltpu.VMEM),
             pl.BlockSpec(memory_space=pltpu.VMEM),
             pl.BlockSpec(memory_space=pl.ANY),
+            pl.BlockSpec(memory_space=pl.ANY),
         ],
         out_specs=pl.BlockSpec(memory_space=pl.ANY),
-        out_shape=jax.ShapeDtypeStruct(sent.shape, jnp.float32),
+        out_shape=jax.ShapeDtypeStruct(whole, jnp.float32),
         scratch_shapes=[
             pltpu.VMEM(sent.shape, jnp.float32),
             pltpu.VMEM(sent.shape, jnp.float32),
+            pltpu.VMEM(whole, jnp.float32),
             pltpu.VMEM((total_z * columns, total_y), jnp.bfloat16),
             pltpu.VMEM((total_z * columns, total_y), jnp.bfloat16),
             pltpu.VMEM((total_z, columns, rows), jnp.float32),
+            pltpu.SemaphoreType.DMA,
             pltpu.SemaphoreType.DMA((components,)),
             pltpu.SemaphoreType.DMA((components,)),
             pltpu.SemaphoreType.DMA((components,)),
@@ -392,7 +429,7 @@
         compiler_params=pltpu.CompilerParams(
             collective_id=0, has_side_effects=True, vmem_limit_bytes=48 * 2**20
         ),
-    )(inverse_z, high, low, sent)
+    )(inverse_z, high, low, early, sent)
 
 
 def turn_body(back_ref, out_ref):
@@ -417,17 +454,26 @@
 def shards_exchange(adjoint, source, jacobian, inverse_x, inverse_y, inverse_z):
     groups = lax.axis_size("grp")
     lines = lax.axis_size("line")
-    rims = rims_of(adjoint)
-    sent = residual_sweep(
-        jacobian, *split_halves(inverse_x), source, adjoint, rims, groups * lines
-    )
-    back = middle(inverse_z, *split_halves(inverse_y), sent, groups, lines)
+    count = lines - 1
+    rows, depth = adjoint.shape[2], adjoint.shape[1]
+    before = lax.ppermute(adjoint[:, :, rows - 8 :], "line", [(i, i + 1) for i in range(count)])
+    after = lax.ppermute(adjoint[:, :, :8], "line", [(i + 1, i) for i in range(count)])
+    below = lax.ppermute(adjoint[:, depth - 2 :], "grp", [(i, i + 1) for i in range(groups - 1)])
+    head, below = lax.optimization_barrier((adjoint[:, :2], below))
+    above = lax.ppermute(head, "grp", [(i + 1, i) for i in range(groups - 1)])
+    split_x = split_halves(inverse_x)
+    first = (below, adjoint, before, after)
+    sent = residual_sweep(0, jacobian, *split_x, source, first, (), groups * lines)
+    early = spread(sent, groups, lines)
+    second = (adjoint, above, before, after)
+    sent = residual_sweep(1, jacobian, *split_x, source, second, (early,), groups * lines)
+    back = middle(inverse_z, *split_halves(inverse_y), early, sent, groups, lines)
     return turn(back)
 
 
 def shards(adjoint, source, jacobian, inverse_x, inverse_y, inverse_z):
     devices = lax.axis_size("grp") * lax.axis_size("line")
-    whole_tiles = adjoint.shape[2] % 128 == 0 and (adjoint.shape[3] // devices) % 16 == 0
+    whole_tiles = adjoint.shape[2] % 128 == 0 and (adjoint.shape[3] // devices) % 16 == 0 and adjoint.shape[1] == 4
     chosen = shards_exchange if whole_tiles else shards_plain
     return chosen(adjoint, source, jacobian, inverse_x, inverse_y, inverse_z)
 

time: 780 us -> 705 us (0.904)
  starting transfers between devices: 81.4 us -> 11 us
  Pallas kernels: 531 us -> 572 us
  waiting for transfers between devices: 130 us -> 98.9 us
  other arithmetic: 20.3 us -> 5.98 us
    pallas_call x1 -> x3, Pallas kernels: 63.7 us -> 223 us  [the longest x1 153 us: spread(): pl.pallas_call(functools.partial(spread_body, groups, lines), in_specs=[p...]
    pallas_call x1, Pallas kernels: 462 us -> 344 us  [middle(): pl.pallas_call(functools.partial(middle_body, groups, lines), in_specs=[p...]
    ppermute x10 -> x4, starting transfers between devices: 81.4 us -> 11 us  [the longest x1 4.05 us: shards_exchange(): lax.ppermute(adjoint[:, :, rows - 8:], 'line', [(i, i + 1) for i in range...]
    ppermute x10 -> x4, waiting for transfers between devices: 130 us -> 98.9 us  [the longest x1 98.9 us: shards_exchange(): lax.ppermute(adjoint[:, depth - 2:], 'grp', [(i, i + 1) for i in range(gr...]
    concatenate x2 -> x0, other arithmetic: 9.35 us -> none  [relayed(): return jnp.concatenate([direct, jnp.where(mine, side, rest)], axis=-1)]
  transfers between devices with their start and end apart: 10 -> 4, of which waited for: 3 -> 1; matrix products, arithmetic and copies ran while one was open for 3% -> 1% of each run, Pallas kernels for 0% -> 27%
where the time goes in v2:
time: 705 us; the launch traced here: 704 us
  Pallas kernels  572 us (81%)
  waiting for transfers between devices  98.9 us (14%)
  local copies, waits for them, and re-layouts  15.9 us (2%)
  starting transfers between devices  11 us (2%)
    pallas_call x1, Pallas kernels, middle(): pl.pallas_call(functools.partial(middle_body, groups, lines), in_specs=[p...  344 us
    pallas_call x1, Pallas kernels, spread(): pl.pallas_call(functools.partial(spread_body, groups, lines), in_specs=[p...  153 us
    ppermute x1, waiting for transfers between devices, shards_exchange(): lax.ppermute(adjoint[:, depth - 2:], 'grp', [(i, i + 1) for i in range(gr...  98.9 us
    pallas_call x2, Pallas kernels, residual_sweep(): pl.pallas_call(functools.partial(residual_sweep_body, pair), grid=(compon...  69.6 us
  transfers between devices with their start and end apart: 4, of which 1 were waited for; matrix products, arithmetic and copies ran while one was open for 1% of the time, Pallas kernels for 27%

profile of v2, /device:TPU:11, one launch (start us, length us, event | category | flops | bytes accessed | tf_op | source)
XLA Modules:
  0.0 704.2 jit_solution(8575996003284777405)
XLA Ops:
  0.0 0.0 copy-start.8
  0.0 8.1 %fusion.3 = (f32[5,2,128,1024]{3,2,1,0:T(8,128)S(1)}, f32[5,2,128,1024]{3,2,1,0:T(8,128)}) fusion(f32[5,4,128,1024]{3,2,1,0:T(8,128)} %first_ref.1), kind=kLoop, calls=%fused_computation.7 | loop fusion | bytes 20971520 | tf_op jit(solution)/shard_map/slice | solution.py:461
  8.1 3.1 collective-permute-start
  11.2 1.4 fusion.2
  12.6 4.0 collective-permute-start.1
  16.7 1.9 collective-permute-start.2
  18.6 0.0 copy-done.8
  18.6 0.0 copy-start.7
  18.6 3.1 fusion.1
  21.7 0.4 copy-done.7
  22.1 0.0 copy-start.1
  22.1 2.9 fusion
  25.0 98.9 %collective-permute-done.first_ref = f32[5,2,128,1024]{3,2,1,0:T(8,128)S(1)} collective-permute-done((f32[5,2,128,1024]{3,2,1,0:T(8,128)S(1)}, f32[5,2,128,1024]{3,2,1,0:T(8,128)S(1)}, u32[]{:S(2)}, u32[]{:S(2)}) %collective-permute-start) | collective-permute-done | bytes 5242912 | tf_op jit(solution)/shard_map/ppermute | solution.py:461
  123.9 0.0 copy-start.6
  123.9 1.9 collective-permute-start.3
  125.8 0.0 collective-permute-done.1.before_ref
  125.8 0.0 collective-permute-done.2.after_ref
  125.8 0.0 copy-done.1
  125.8 0.4 copy-done.6
  126.3 34.5 %shard_map.64.sent_ref = f32[5,32,2,32,128]{4,3,2,1,0:T(8,128)} custom-call(f32[3,5,5]{2,1,0:T(8,128)S(1)} %copy.7.jacobian_ref, bf16[1024,1024]{1,0:T(8,128)(2,1)S(1)} %get-tuple-element.14.high_ref, bf16[1024,1024]{1,0:T(8,128)(2,1)S(1)} %get-tuple-element.13.low_ref, f32[5,4,128,1024]{3,2,1,0:T(8,128)} %source_ref.3, f32[5,2,128,1024]{3,2,1,0:T(8,128)} %copy-done.6, ...), custom_call_target="tpu_custom_call" | custom-call | tf_op jit(solution)/shard_map/pallas_call | solution.py:223
  160.8 152.9 %shard_map.65.rest_0_.early_ref = f32[5,32,2,32,128]{4,3,2,1,0:T(8,128)} custom-call(f32[5,32,2,32,128]{4,3,2,1,0:T(8,128)} %shard_map.64.sent_ref), custom_call_target="tpu_custom_call" | custom-call | flops 99999997952 | bytes 10485760 | tf_op jit(solution)/shard_map/pallas_call | solution.py:291
  313.7 0.0 collective-permute-done.3.second_ref
  313.7 0.0 copy-start.2
  313.7 1.6 copy-done.2
  315.3 35.1 %shard_map.66.sent_ref = f32[5,32,2,32,128]{4,3,2,1,0:T(8,128)} custom-call(f32[3,5,5]{2,1,0:T(8,128)S(1)} %copy.7.jacobian_ref, bf16[1024,1024]{1,0:T(8,128)(2,1)S(1)} %copy-done.2, bf16[1024,1024]{1,0:T(8,128)(2,1)S(1)} %get-tuple-element.13.low_ref, f32[5,4,128,1024]{3,2,1,0:T(8,128)} %source_ref.3, f32[5,4,128,1024]{3,2,1,0:T(8,128)} %first_ref.1, ...), custom_call_target="tpu_custom_call" | custom-call | tf_op jit(solution)/shard_map/pallas_call | solution.py:223
  350.4 0.0 copy-done.3
  350.5 0.0 copy-done.4
  350.5 0.0 copy-done.5
  350.5 344.0 %shard_map.67.back_ref = f32[5,32,4,32,128]{4,3,2,1,0:T(8,128)} custom-call(f32[16,16]{1,0:T(8,128)S(1)} %copy-done.5, bf16[1024,1024]{1,0:T(8,128)(2,1)S(1)} %copy-done.4, bf16[1024,1024]{1,0:T(8,128)(2,1)S(1)} %copy-done.3, f32[5,32,2,32,128]{4,3,2,1,0:T(8,128)} %shard_map.65.rest_0_.early_ref, f32[5,32,2,32,128]{4,3,2,1,0:T(8,128)} %shard_map.66.sent_ref), custom_call_target="tpu_custom_call" | custom-call | tf_op jit(solution)/shard_map/pallas_call | solution.py:405
  694.5 0.0 copy-start
  694.5 4.0 copy-done
  698.4 5.8 shard_map.68
  (4 shorter events, 0.0 us)
Async XLA Ops:
  0.0 18.6 %copy-start.8 = (f32[3,5,5]{2,0,1:T(4,128)S(1)}, f32[3,5,5]{2,0,1:T(4,128)}, u32[]{:S(2)}) copy-start(f32[3,5,5]{2,0,1:T(4,128)} %param.8) | copy-start | bytes 904
  8.1 115.8 %collective-permute-start = (f32[5,2,128,1024]{3,2,1,0:T(8,128)S(1)}, f32[5,2,128,1024]{3,2,1,0:T(8,128)S(1)}, u32[]{:S(2)}, u32[]{:S(2)}) collective-permute-start(f32[5,2,128,1024]{3,2,1,0:T(8,128)S(1)} %get-tuple-element.11), channel_id=1, source_target_pairs={{0,8},{8,16},{16,24},{1,9},{9,17},{17,25},{2,10},{10,18},{18,26},{... | collective-permute-start | bytes 15728648 | tf_op jit(solution)/shard_map/ppermute | solution.py:461
  12.6 113.2 %collective-permute-start.1 = (f32[5,4,8,1024]{3,2,1,0:T(8,128)S(1)}, f32[5,4,8,1024]{3,2,1,0:T(8,128)S(1)}, u32[]{:S(2)}, u32[]{:S(2)}) collective-permute-start(f32[5,4,8,1024]{3,2,1,0:T(8,128)S(1)} %get-tuple-element.10), channel_id=1, source_target_pairs={{0,1},{1,2},{2,3},{3,4},{4,5},{5,6},{6,7},{8,9},{9,10},{10,11},{11... | collective-permute-start | bytes 1966088 | tf_op jit(solution)/shard_map/ppermute | solution.py:459
  16.7 109.1 %collective-permute-start.2 = (f32[5,4,8,1024]{3,2,1,0:T(8,128)S(1)}, f32[5,4,8,1024]{3,2,1,0:T(8,128)S(1)}, u32[]{:S(2)}, u32[]{:S(2)}) collective-permute-start(f32[5,4,8,1024]{3,2,1,0:T(8,128)S(1)} %get-tuple-element.9), channel_id=1, source_target_pairs={{1,0},{2,1},{3,2},{4,3},{5,4},{6,5},{7,6},{9,8},{10,9},{11,10},{12... | collective-permute-start | bytes 1966088 | tf_op jit(solution)/shard_map/ppermute | solution.py:460
  18.6 3.5 copy-start.7
  22.1 103.7 %copy-start.1 = (bf16[1024,1024]{1,0:T(8,128)(2,1)}, bf16[1024,1024]{1,0:T(8,128)(2,1)S(1)}, u32[]{:S(2)}) copy-start(bf16[1024,1024]{1,0:T(8,128)(2,1)S(1)} %get-tuple-element.14.high_ref) | copy-start | bytes 6291460
  123.9 2.4 copy-start.6
  123.9 189.8 %collective-permute-start.3 = (f32[5,2,128,1024]{3,2,1,0:T(8,128)}, f32[5,2,128,1024]{3,2,1,0:T(8,128)}, u32[]{:S(2)}, u32[]{:S(2)}) collective-permute-start(f32[5,2,128,1024]{3,2,1,0:T(8,128)} %get-tuple-element.8), channel_id=1, source_target_pairs={{8,0},{16,8},{24,16},{9,1},{17,9},{25,17},{10,2},{18,10},{26,18},{... | collective-permute-start | bytes 15728648 | tf_op jit(solution)/shard_map/ppermute | solution.py:463
  313.7 1.6 copy-start.2
  315.3 35.1 %copy-start.3 = (bf16[1024,1024]{1,0:T(8,128)(2,1)S(1)}, bf16[1024,1024]{1,0:T(8,128)(2,1)}, u32[]{:S(2)}) copy-start(bf16[1024,1024]{1,0:T(8,128)(2,1)} %get-tuple-element.15.low_ref) | copy-start | bytes 6291460
  315.3 35.1 %copy-start.4 = (bf16[1024,1024]{1,0:T(8,128)(2,1)S(1)}, bf16[1024,1024]{1,0:T(8,128)(2,1)}, u32[]{:S(2)}) copy-start(bf16[1024,1024]{1,0:T(8,128)(2,1)} %get-tuple-element.16.high_ref) | copy-start | bytes 6291460
  315.3 35.1 %copy-start.5 = (f32[16,16]{1,0:T(8,128)S(1)}, f32[16,16]{1,0:T(8,128)}, u32[]{:S(2)}) copy-start(f32[16,16]{1,0:T(8,128)} %z_ref.1) | copy-start | bytes 3076
  694.5 4.0 copy-start

commit v3 on v2

--- a/solution.py
+++ b/solution.py
@@ -263,17 +263,28 @@
     return own_g, own_l, partner
 
 
-def spread_body(groups, lines, sent_ref, got_ref, send_sem, recv_sem):
-    components, devices = sent_ref.shape[:2]
-    own_g, own_l, partner = meet(groups, lines)
+def sweep_spread_body(groups, lines, *refs):
+    inputs, got_ref = refs[:8], refs[8]
+    padded, residual, sems, sent, send_sem, recv_sem = refs[9:]
+    components, devices = sent.shape[:2]
+    v = pl.program_id(0)
+    own_g = lax.axis_index("grp")
+    own_l = lax.axis_index("line")
     own = own_g * lines + own_l
-    pltpu.make_async_copy(sent_ref.at[:, own], got_ref.at[:, own], recv_sem).start()
+
+    @pl.when(v == 0)
+    def _():
+        meet(groups, lines)
+
+    residual_sweep_body(0, *inputs, sent.at[pl.ds(v, 1)], padded, residual, sems)
+    pltpu.make_async_copy(sent.at[v, own], got_ref.at[v, own], recv_sem).start()
 
     def one(step, c):
-        g, l = partner(step)
+        l = lax.rem(own_l + step // groups, lines)
+        g = lax.rem(own_g + step % groups, groups)
         pltpu.make_async_remote_copy(
-            src_ref=sent_ref.at[:, g * lines + l],
-            dst_ref=got_ref.at[:, own],
+            src_ref=sent.at[v, g * lines + l],
+            dst_ref=got_ref.at[v, own],
             send_sem=send_sem,
             recv_sem=recv_sem,
             device_id=(g, l),
@@ -282,23 +293,45 @@
         return c
 
     lax.fori_loop(1, devices, one, 0)
-    others = pl.ds(0, devices - 1)
-    pltpu.make_async_copy(sent_ref.at[:, others], sent_ref.at[:, others], send_sem).wait()
-    pltpu.make_async_copy(got_ref, got_ref, recv_sem).wait()
-
-
-def spread(sent, groups, lines):
+
+    @pl.when(v == components - 1)
+    def _():
+        others = sent.at[:, pl.ds(0, devices - 1)]
+        pltpu.make_async_copy(others, others, send_sem).wait()
+        pltpu.make_async_copy(got_ref, got_ref, recv_sem).wait()
+
+
+def sweep_spread(jacobian, high, low, source, parts, groups, lines):
+    components, depth, rows, width = source.shape
+    depth = depth // 2
+    devices = groups * lines
+    shape = (components, devices, depth, width // devices, rows)
+    once = pl.Buffered(1)
     return pl.pallas_call(
-        functools.partial(spread_body, groups, lines),
-        in_specs=[pl.BlockSpec(memory_space=pl.ANY)],
+        functools.partial(sweep_spread_body, groups, lines),
+        grid=(components,),
+        in_specs=[
+            pl.BlockSpec(memory_space=pltpu.SMEM),
+            pl.BlockSpec((width, width), lambda v: (0, 0), pipeline_mode=once),
+            pl.BlockSpec((width, width), lambda v: (0, 0), pipeline_mode=once),
+            pl.BlockSpec((1, depth, rows, width), lambda v: (v, 0, 0, 0)),
+        ]
+        + [pl.BlockSpec(memory_space=pl.ANY)] * len(parts),
         out_specs=pl.BlockSpec(memory_space=pl.ANY),
-        out_shape=jax.ShapeDtypeStruct(sent.shape, jnp.float32),
-        scratch_shapes=[pltpu.SemaphoreType.DMA, pltpu.SemaphoreType.DMA],
-        cost_estimate=pl.CostEstimate(
-            flops=10**11, bytes_accessed=2 * sent.size * 4, transcendentals=0
+        out_shape=jax.ShapeDtypeStruct(shape, jnp.float32),
+        scratch_shapes=[
+            pltpu.VMEM((components, depth + 4, rows + 16, width), jnp.float32),
+            pltpu.VMEM((depth * rows, width), jnp.float32),
+            pltpu.SemaphoreType.DMA((4,)),
+            pltpu.VMEM(shape, jnp.float32),
+            pltpu.SemaphoreType.DMA,
+            pltpu.SemaphoreType.DMA,
+        ],
+        cost_estimate=pl.CostEstimate(flops=10**11, bytes_accessed=10**8, transcendentals=0),
+        compiler_params=pltpu.CompilerParams(
+            collective_id=1, has_side_effects=True, vmem_limit_bytes=48 * 2**20
         ),
-        compiler_params=pltpu.CompilerParams(collective_id=1, has_side_effects=True),
-    )(sent)
+    )(jacobian, high, low, source, *parts)
 
 
 def middle_body(
@@ -463,8 +496,7 @@
     above = lax.ppermute(head, "grp", [(i + 1, i) for i in range(groups - 1)])
     split_x = split_halves(inverse_x)
     first = (below, adjoint, before, after)
-    sent = residual_sweep(0, jacobian, *split_x, source, first, (), groups * lines)
-    early = spread(sent, groups, lines)
+    early = sweep_spread(jacobian, *split_x, source, first, groups, lines)
     second = (adjoint, above, before, after)
     sent = residual_sweep(1, jacobian, *split_x, source, second, (early,), groups * lines)
     back = middle(inverse_z, *split_halves(inverse_y), early, sent, groups, lines)

time: 705 us -> 691 us (0.980)
  Pallas kernels: 572 us -> 557 us
    pallas_call x2 -> x1, Pallas kernels: 69.6 us -> 34.5 us  [residual_sweep(): pl.pallas_call(functools.partial(residual_sweep_body, pair), grid=(compon...]
    pallas_call x1, Pallas kernels: 153 us -> 172 us  [sweep_spread(): pl.pallas_call(functools.partial(sweep_spread_body, groups, lines), grid=...]
  transfers between devices with their start and end apart: 4 -> 4, of which waited for: 1 -> 1; matrix products, arithmetic and copies ran while one was open for 1% -> 0% of each run, Pallas kernels for 27% -> 25%
where the time goes in v3:
time: 691 us; the launch traced here: 690 us
  Pallas kernels  557 us (81%)
  waiting for transfers between devices  102 us (15%)
  local copies, waits for them, and re-layouts  17.4 us (3%)
  starting transfers between devices  11 us (2%)
    pallas_call x1, Pallas kernels, middle(): pl.pallas_call(functools.partial(middle_body, groups, lines), in_specs=[p...  345 us
    pallas_call x1, Pallas kernels, sweep_spread(): pl.pallas_call(functools.partial(sweep_spread_body, groups, lines), grid=...  172 us
    ppermute x1, waiting for transfers between devices, shards_exchange(): lax.ppermute(adjoint[:, depth - 2:], 'grp', [(i, i + 1) for i in range(gr...  102 us
    pallas_call x1, Pallas kernels, residual_sweep(): pl.pallas_call(functools.partial(residual_sweep_body, pair), grid=(compon...  34.5 us
  transfers between devices with their start and end apart: 4, of which 1 were waited for; matrix products, arithmetic and copies ran while one was open for 0% of the time, Pallas kernels for 25%

profile of v3, /device:TPU:11, one launch (start us, length us, event | category | flops | bytes accessed | tf_op | source)
XLA Modules:
  0.0 690.1 jit_solution(14855982774201561923)
XLA Ops:
  0.0 0.0 copy-start.4
  0.0 0.0 copy-start.2
  0.0 10.4 %fusion.3 = (f32[5,2,128,1024]{3,2,1,0:T(8,128)}, f32[5,2,128,1024]{3,2,1,0:T(8,128)}) fusion(f32[5,4,128,1024]{3,2,1,0:T(8,128)} %first_ref.1), kind=kLoop, calls=%fused_computation.7 | loop fusion | bytes 20971520 | tf_op jit(solution)/shard_map/slice | solution.py:494
  10.4 3.1 collective-permute-start
  13.5 1.4 fusion.2
  14.9 4.0 collective-permute-start.1
  19.0 1.9 collective-permute-start.2
  20.9 0.0 copy-done.4
  20.9 0.0 copy-done.2
  20.9 0.0 copy-start.3
  20.9 0.9 fusion.1
  21.9 1.2 copy-done.3
  23.1 0.9 fusion
  24.1 102.4 %collective-permute-done.refs_4_ = f32[5,2,128,1024]{3,2,1,0:T(8,128)S(1)} collective-permute-done((f32[5,2,128,1024]{3,2,1,0:T(8,128)}, f32[5,2,128,1024]{3,2,1,0:T(8,128)S(1)}, u32[]{:S(2)}, u32[]{:S(2)}) %collective-permute-start) | collective-permute-done | bytes 5242912 | tf_op jit(solution)/shard_map/ppermute | solution.py:494
  126.4 0.0 copy-start.5
  126.4 1.9 collective-permute-start.3
  128.3 0.0 collective-permute-done.1.refs_6_.before_ref
  128.4 0.0 collective-permute-done.2.refs_7_.after_ref
  128.4 0.4 copy-done.5
  128.8 171.8 %shard_map.64.rest_0_.early_ref = f32[5,32,2,32,128]{4,3,2,1,0:T(8,128)} custom-call(f32[3,5,5]{2,1,0:T(8,128)S(1)} %copy.7.refs_0_.jacobian_ref, bf16[1024,1024]{1,0:T(8,128)(2,1)S(1)} %get-tuple-element.14.refs_1_.high_ref, bf16[1024,1024]{1,0:T(8,128)(2,1)S(1)} %get-tuple-element.13.refs_2_.low_ref, f32[5,4,128,1024]{3,2,1,0:T(8,128)} %source_ref.1, ...), custom_call_target="tpu_custom_call" | custom-call | flops 99999997952 | bytes 100000000 | tf_op jit(solution)/shard_map/pallas_call | solution.py:310
  300.6 0.0 copy-start.1
  300.6 0.0 collective-permute-done.3.second_ref
  300.6 34.5 %shard_map.65.sent_ref = f32[5,32,2,32,128]{4,3,2,1,0:T(8,128)} custom-call(f32[3,5,5]{2,1,0:T(8,128)S(1)} %copy.7.refs_0_.jacobian_ref, bf16[1024,1024]{1,0:T(8,128)(2,1)S(1)} %get-tuple-element.14.refs_1_.high_ref, bf16[1024,1024]{1,0:T(8,128)(2,1)S(1)} %get-tuple-element.13.refs_2_.low_ref, f32[5,4,128,1024]{3,2,1,0:T(8,128)} %source_ref.1, ...), custom_call_target="tpu_custom_call" | custom-call | tf_op jit(solution)/shard_map/pallas_call | solution.py:223
  335.1 0.0 copy-done.1
  335.1 345.2 %shard_map.66.back_ref = f32[5,32,4,32,128]{4,3,2,1,0:T(8,128)} custom-call(f32[16,16]{1,0:T(8,128)S(1)} %copy-done.1, bf16[1024,1024]{1,0:T(8,128)(2,1)S(1)} %get-tuple-element.16.high_ref, bf16[1024,1024]{1,0:T(8,128)(2,1)S(1)} %get-tuple-element.15.low_ref, f32[5,32,2,32,128]{4,3,2,1,0:T(8,128)} %shard_map.64.rest_0_.early_ref, ...), custom_call_target="tpu_custom_call" | custom-call | tf_op jit(solution)/shard_map/pallas_call | solution.py:438
  680.4 0.0 copy-start
  680.4 4.0 copy-done
  684.4 5.8 shard_map.67
  (1 shorter events, 0.0 us)
Async XLA Ops:
  0.0 20.9 %copy-start.4 = (f32[3,5,5]{2,0,1:T(4,128)S(1)}, f32[3,5,5]{2,0,1:T(4,128)}, u32[]{:S(2)}) copy-start(f32[3,5,5]{2,0,1:T(4,128)} %param.8) | copy-start | bytes 904
  0.0 20.9 %copy-start.2 = (f32[1024,1024]{1,0:T(8,128)S(1)}, f32[1024,1024]{1,0:T(8,128)}, u32[]{:S(2)}) copy-start(f32[1024,1024]{1,0:T(8,128)} %param.9) | copy-start | bytes 12582916
  10.4 116.0 %collective-permute-start = (f32[5,2,128,1024]{3,2,1,0:T(8,128)}, f32[5,2,128,1024]{3,2,1,0:T(8,128)S(1)}, u32[]{:S(2)}, u32[]{:S(2)}) collective-permute-start(f32[5,2,128,1024]{3,2,1,0:T(8,128)} %get-tuple-element.11), channel_id=1, source_target_pairs={{0,8},{8,16},{16,24},{1,9},{9,17},{17,25},{2,10},{10,18},{18,26},{... | collective-permute-start | bytes 15728648 | tf_op jit(solution)/shard_map/ppermute | solution.py:494
  14.9 113.4 %collective-permute-start.1 = (f32[5,4,8,1024]{3,2,1,0:T(8,128)S(1)}, f32[5,4,8,1024]{3,2,1,0:T(8,128)S(1)}, u32[]{:S(2)}, u32[]{:S(2)}) collective-permute-start(f32[5,4,8,1024]{3,2,1,0:T(8,128)S(1)} %get-tuple-element.10), channel_id=1, source_target_pairs={{0,1},{1,2},{2,3},{3,4},{4,5},{5,6},{6,7},{8,9},{9,10},{10,11},{11... | collective-permute-start | bytes 1966088 | tf_op jit(solution)/shard_map/ppermute | solution.py:492
  19.0 109.4 %collective-permute-start.2 = (f32[5,4,8,1024]{3,2,1,0:T(8,128)S(1)}, f32[5,4,8,1024]{3,2,1,0:T(8,128)S(1)}, u32[]{:S(2)}, u32[]{:S(2)}) collective-permute-start(f32[5,4,8,1024]{3,2,1,0:T(8,128)S(1)} %get-tuple-element.9), channel_id=1, source_target_pairs={{1,0},{2,1},{3,2},{4,3},{5,4},{6,5},{7,6},{9,8},{10,9},{11,10},{12... | collective-permute-start | bytes 1966088 | tf_op jit(solution)/shard_map/ppermute | solution.py:493
  20.9 2.2 copy-start.3
  126.4 2.4 copy-start.5
  126.4 174.2 %collective-permute-start.3 = (f32[5,2,128,1024]{3,2,1,0:T(8,128)}, f32[5,2,128,1024]{3,2,1,0:T(8,128)}, u32[]{:S(2)}, u32[]{:S(2)}) collective-permute-start(f32[5,2,128,1024]{3,2,1,0:T(8,128)} %get-tuple-element.8), channel_id=1, source_target_pairs={{8,0},{16,8},{24,16},{9,1},{17,9},{25,17},{10,2},{18,10},{26,18},{... | collective-permute-start | bytes 15728648 | tf_op jit(solution)/shard_map/ppermute | solution.py:496
  300.6 34.5 %copy-start.1 = (f32[16,16]{1,0:T(8,128)S(1)}, f32[16,16]{1,0:T(8,128)}, u32[]{:S(2)}) copy-start(f32[16,16]{1,0:T(8,128)} %z_ref.1) | copy-start | bytes 3076
  680.4 4.0 copy-start
